TPU v7x, 128 devices: a whole 4x4x4 slice. The times are simulated.
128 devices in a mesh: occ: 4 (over z), vir: 32 (over x, y, core).
Axes of the slice: x: 4, y: 4, z: 4, core: 2. Of those that a mesh axis runs over, the one named last changes fastest.
Arguments:
- amps: bfloat16 [3072, 16384], P('occ', 'vir'), may hold values from -6 to 6
- cycle_amps: bfloat16 [3072, 8192], P(('occ', 'vir')), may hold values from -6 to 6
- cycle_ints: bfloat16 [8192, 16384], P(None, 'vir'), may hold values from -0.0625 to 0.0625
- ladder_ints: bfloat16 [64, 4, 256, 256], P('vir'), may hold values from -0.1875 to 0.1875
- sources: int32 [64, 4], replicated, may hold values from 0 to 63, as said below
- counts: int32 [64], replicated, may hold values from 1 to 4
- eps_occ: float32 [3072], P('occ'), may hold values from 0.5 to 4
- eps_vir: float32 [16384], P('vir'), may hold values from 0.5 to 4
Outputs:
- residual: bfloat16 [3072, 16384], P('occ', 'vir')
- new_amps: bfloat16 [3072, 16384], P('occ', 'vir')
- residual_norm: float32 [], replicated
Inputs may be any that keep to these rules, and one draw needn't show every extreme that they name: `sources`: with owner(s) = s // 2: for each group of 2 consecutive target tiles (those of one owner), all 8 entries of their rows name tiles of different owners.
All inputs are finite; a program needn't handle non-finite values.
Results may differ from a plain program's by a relative error of at most 0.012.
Values may be sent and summed in bfloat16 or wider, within the bound.
A program may use at most 128 MiB of HBM per device.

v0:
```python
import jax
import jax.numpy as jnp
from jax import lax
from jax.sharding import PartitionSpec as P


def add_block(totals, column_block, weight, inside):
    return lax.cond(
        inside,
        lambda run: run + jnp.dot(column_block, weight, preferred_element_type=jnp.float32),
        lambda run: run,
        totals,
    )


def on_device(amps, cycle_amps, cycle_ints, ladder_ints, sources, counts, eps_occ, eps_vir):
    my_index = lax.axis_index("vir")
    owned = ladder_ints.shape[0]
    slots = ladder_ints.shape[1]
    tile_width = ladder_ints.shape[2]
    cycle = jnp.dot(
        lax.all_gather(cycle_amps, "vir", axis=0, tiled=True),
        cycle_ints,
        preferred_element_type=jnp.float32,
    ).astype(jnp.bfloat16)
    dressed = (amps.astype(jnp.float32) + cycle.astype(jnp.float32)).astype(jnp.bfloat16)
    rows = dressed.shape[0]
    local_sources = lax.dynamic_slice_in_dim(sources, my_index * owned, owned, 0)
    live_counts = lax.dynamic_slice_in_dim(counts, my_index * owned, owned, 0)
    starting = tuple((jnp.zeros((rows, tile_width), jnp.float32) for target_slot in range(owned)))
    shard_piece = lax.all_gather(dressed, "vir", axis=1, tiled=True)
    span_width = shard_piece.shape[1]
    updated = []
    for target_slot in range(owned):
        totals = starting[target_slot]
        for source_slot in range(slots):
            column = local_sources[target_slot, source_slot] * tile_width
            inside = (
                (column >= 0) & (column < span_width) & (source_slot < live_counts[target_slot])
            )
            offset = jnp.clip(column, 0, span_width - tile_width)
            column_block = lax.dynamic_slice_in_dim(shard_piece, offset, tile_width, 1)
            totals = add_block(totals, column_block, ladder_ints[target_slot, source_slot], inside)
        updated.append(totals)
    ladder_parts = tuple(updated)
    ladder = jnp.concatenate(ladder_parts, axis=1)
    residual = (ladder + cycle.astype(jnp.float32)).astype(jnp.bfloat16)
    res_wide = residual.astype(jnp.float32)
    denom = eps_occ[:, None] + eps_vir[None, :]
    new_amps = (amps.astype(jnp.float32) - res_wide / denom).astype(jnp.bfloat16)
    residual_norm = lax.psum(jnp.sum(res_wide * res_wide), ("occ", "vir"))
    return (residual, new_amps, residual_norm)


def solution(mesh):
    placed = (
        P("occ", "vir"),
        P(("occ", "vir"), None),
        P(None, "vir"),
        P("vir", None, None, None),
        P(),
        P(),
        P("occ"),
        P("vir"),
    )
    return jax.shard_map(
        on_device,
        mesh=mesh,
        in_specs=placed,
        out_specs=(P("occ", "vir"), P("occ", "vir"), P()),
        check_vma=False,
    )
```

profile of v0, /device:TPU:1, one launch (start us, length us, event | category | flops | bytes accessed | tf_op | source)
XLA Modules:
  0.0 278.3 jit_solution(2381505477691194744)
XLA Ops:
  7.2 0.0 copy-start
  7.2 0.0 all-gather.3.cloned.1.call-start
  7.2 0.7 all-gather.3.cloned.1.call-update
  7.9 0.0 copy-start.6
  7.9 0.0 copy-start.2
  7.9 0.0 all-gather.5.cloned.1.call-start
  8.0 68.7 %all-gather.3.cloned.1.call-done = bf16[768,8192]{1,0:T(8,128)(2,1)} async-done(((bf16[24,8192]{1,0:T(8,128)(2,1)}), bf16[768,8192]{1,0:T(8,128)(2,1)}) %all-gather.3.cloned.1.call-update) | async-done | bytes 12582928 | tf_op jit(solution)/shard_map/all_gather | solution.py:22
  76.7 13.0 %fusion.35 = (bf16[768,512]{1,0:T(8,128)(2,1)}, bf16[768,512]{1,0:T(8,128)(2,1)}) fusion(bf16[768,512]{1,0:T(8,128)(2,1)} %param.24, bf16[768,8192]{1,0:T(8,128)(2,1)} %all-gather.3.cloned.1.call-done, bf16[8192,512]{1,0:T(8,128)(2,1)} %param.26), kind=kOutput, calls=%fused_computation.46 | convolution fusion | flops 6444417024 | bytes 23330816 | tf_op jit(solution)/shard_map/dot_general | solution.py:21
  89.7 0.0 all-gather.5.cloned.1.call-update
  89.8 0.0 copy-done
  89.8 0.1 constant_dynamic-slice_fusion
  89.8 0.6 fusion.39
  93.6 0.0 copy-done.6
  93.6 0.1 dynamic_slice.37
  93.7 0.6 fusion.40
  101.3 91.2 %all-gather.5.cloned.1.call-done = bf16[768,16384]{1,0:T(8,128)(2,1)} async-done(((bf16[768,512]{1,0:T(8,128)(2,1)}), bf16[768,16384]{1,0:T(8,128)(2,1)}) %all-gather.5.cloned.1.call-update) | async-done | bytes 25165840 | tf_op jit(solution)/shard_map/all_gather | solution.py:31
  192.5 0.0 copy-done.2
  192.5 1.4 conditional.8
  192.5 1.4 fusion.8
  193.9 1.4 conditional.9
  193.9 1.4 convolution_add_fusion.2
  195.3 0.0 copy-start.3
  195.3 0.0 copy-start.4
  195.3 0.0 copy-start.5
  195.3 1.5 conditional.10
  195.4 1.5 convolution_add_fusion.3
  196.9 1.4 conditional.12
  196.9 1.4 fusion.21
  198.3 1.4 conditional.13
  198.3 1.4 convolution_add_fusion.4
  199.7 1.4 conditional.14
  199.7 1.4 convolution_add_fusion.5
  201.2 2.2 fusion.37
  203.3 0.0 copy-start.1
  203.3 66.8 %psum.7 = f32[]{:T(128)} all-reduce(f32[]{:T(128)} %get-tuple-element.273), channel_id=1, replica_groups=mesh['occ'=4,'vir'=32] {'occ','vir'}, use_global_device_ids=true, to_apply=%region_17.18 | all-reduce | flops 1 | bytes 8 | tf_op jit(solution)/shard_map/psum | solution.py:51
  270.1 0.0 copy-done.3
  270.1 0.0 copy-done.4
  270.1 0.0 copy-done.5
  270.1 1.3 fusion.34
  271.4 0.0 copy-done.1
  (2 shorter events, 0.0 us)
Async XLA Ops:
  7.2 82.6 %copy-start = (s32[64,4]{0,1:T(4,128)S(1)}, s32[64,4]{0,1:T(4,128)}, u32[]{:S(2)}) copy-start(s32[64,4]{0,1:T(4,128)} %param.28) | copy-start | bytes 3076
  7.2 69.5 %all-gather.3.cloned.1.call-start = ((), (), s32[]{:S(2)}) async-start(), calls=%async_computation | async-start | bytes 12976128 | tf_op jit(solution)/shard_map/all_gather | solution.py:22
  7.9 85.7 %copy-start.6 = (s32[64]{0:T(128)S(1)}, s32[64]{0:T(128)}, u32[]{:S(2)}) copy-start(s32[64]{0:T(128)} %param.29) | copy-start | bytes 772
  7.9 184.6 %copy-start.2 = (bf16[2,4,256,256]{3,2,1,0:T(8,128)(2,1)S(1)}, bf16[2,4,256,256]{3,2,1,0:T(8,128)(2,1)}, u32[]{:S(2)}) copy-start(bf16[2,4,256,256]{3,2,1,0:T(8,128)(2,1)} %param.27) | copy-start | bytes 3145732
  7.9 184.5 %all-gather.5.cloned.1.call-start = ((), (), s32[]{:S(2)}) async-start(), calls=%async_computation.1 | async-start | bytes 25952256 | tf_op jit(solution)/shard_map/all_gather | solution.py:31
  195.3 74.8 %copy-start.3 = (bf16[768,512]{1,0:T(8,128)(2,1)S(1)}, bf16[768,512]{1,0:T(8,128)(2,1)}, u32[]{:S(2)}) copy-start(bf16[768,512]{1,0:T(8,128)(2,1)} %param.24) | copy-start | bytes 2359300
  195.3 74.8 %copy-start.4 = (f32[768]{0:T(1024)S(1)}, f32[768]{0:T(1024)}, u32[]{:S(2)}) copy-start(f32[768]{0:T(1024)} %param.30) | copy-start | bytes 9220
  195.3 74.8 %copy-start.5 = (f32[512]{0:T(512)S(1)}, f32[512]{0:T(512)}, u32[]{:S(2)}) copy-start(f32[512]{0:T(512)} %param.31) | copy-start | bytes 6148
  203.3 68.1 %copy-start.1 = (bf16[768,512]{1,0:T(8,128)(2,1)}, bf16[768,512]{1,0:T(8,128)(2,1)S(1)}, u32[]{:S(2)}) copy-start(bf16[768,512]{1,0:T(8,128)(2,1)S(1)} %get-tuple-element.274) | copy-start | bytes 2359300
Sparse Core Ops, SparseCore 0:
  10.3 66.3 all-gather.2
  89.9 102.5 all-gather.4
where the time goes:
time: 279 us; the launch traced here: 278 us
  waiting for transfers between devices  161 us (58%)
  blocking collectives  66.8 us (24%)
  between operations  24.3 us (9%)
  matrix products  21.5 us (8%)
  other arithmetic  3.46 us (1%)
    all_gather x1, waiting for transfers between devices, on_device(): shard_piece = lax.all_gather(dressed, 'vir', axis=1, tiled=True)  91.2 us
    all_gather x1, waiting for transfers between devices, on_device(): lax.all_gather(cycle_amps, 'vir', axis=0, tiled=True)  68.7 us
    psum x1, blocking collectives, on_device(): residual_norm = lax.psum(jnp.sum(res_wide * res_wide), ('occ', 'vir'))  66.8 us
    dot_general x1, matrix products, on_device(): jnp.dot(lax.all_gather(cycle_amps, 'vir', axis=0, tiled=True), cycle_ints...  13 us
    dot_general x6, matrix products, add_block(): jnp.dot(column_block, weight, preferred_element_type=jnp.float32)  8.44 us
  transfers between devices with their start and end apart: 2, of which 2 were waited for; matrix products, arithmetic and copies ran while one was open for 1% of the time, Pallas kernels for 0%

commit v1 on v0

v1 whole, which is shorter than its diff:
```python
import functools

import jax
import jax.numpy as jnp
from jax import lax
from jax.experimental import pallas as pl
from jax.experimental.pallas import tpu as pltpu
from jax.sharding import PartitionSpec as P

MESH = pl.DeviceIdType.MESH
RING = 4
DIST = (1, 3, 2)
CAPS = (6, 8, 16)
ORDER = (0, 1, 3, 2)
F32, BF16 = jnp.float32, jnp.bfloat16


def place():
    vir = lax.axis_index("vir")
    core = vir % 2
    y = (vir // 2) % RING
    x = vir // (2 * RING)
    first = jnp.where(core == 0, x, y)
    second = jnp.where(core == 0, y, x)
    return core, first, second, x, y


def tables(sources, counts, sources_v, counts_v, pack, lad, most, before):
    core, p, q, x, y = place()

    def split(tile):
        tx, ty = tile // 16, (tile // 4) % 4
        return jnp.where(core == 0, tx, ty), jnp.where(core == 0, ty, tx), tile % 4

    def asked(chip, line):
        mask = jnp.int32(0)
        for t in range(4):
            for k in range(4):
                tp, tq, tt = split(sources[chip * 4 + t, k])
                hit = (tq == line) & (k < counts[chip * 4 + t])
                mask = mask | jnp.where(hit, jnp.int32(1) << (tp * 4 + tt), 0)
        return mask

    def chip_at(fp, fq):
        return jnp.where(core == 0, fp * 4 + fq, fq * 4 + fp)

    for g, d in enumerate(DIST):
        other = (q + d) % RING
        mask = asked(chip_at(p, other), q)
        for e in range(16):
            pack[g, e] = 0
        n = jnp.int32(0)
        for e in range(16):
            pack[g, n] = e
            n = n + ((mask >> e) & 1)
        mask = asked(chip_at(p, q), other)
        n = jnp.int32(0)
        for e in range(16):
            before[g, e] = n
            n = n + ((mask >> e) & 1)
    mine = x * 4 + y
    for t in range(4):
        for k in range(4):
            tp, tq, tt = split(sources[mine * 4 + t, k])
            live = k < counts[mine * 4 + t]
            local = tq == q
            d = (tq - q + RING) % RING
            g = jnp.where(d == 1, 0, jnp.where(d == 3, 1, 2))
            e = tp * 4 + tt
            slot = t * 4 + k
            lad[0, slot] = jnp.where(live & local, e, p * 4)
            lad[1, slot] = jnp.where(live & ~local, g, 0)
            lad[2, slot] = jnp.where(live & ~local, before[g, e], 0)
            lad[3, slot] = jnp.where(live & ~local, 0, 1)
            lad[4, slot] = jnp.where(live, 1, 0)

    tiles = lax.broadcasted_iota(jnp.int32, (64, 128), 1)
    hits = jnp.zeros((64, 128), F32)
    for k in range(4):
        hits += jnp.where((sources_v[:, k : k + 1] == tiles) & (counts_v[...] > k), 1.0, 0.0)
    group = lax.broadcasted_iota(jnp.int32, (16, 64), 0)
    member = lax.broadcasted_iota(jnp.int32, (16, 64), 1) // 4
    need = jnp.dot(jnp.where(group == member, 1.0, 0.0).astype(BF16), hits.astype(BF16), preferred_element_type=F32)
    need = jnp.minimum(need, 1.0)
    tile = lax.broadcasted_iota(jnp.int32, (128, 128), 0)
    line = lax.broadcasted_iota(jnp.int32, (128, 128), 1)
    inside = ((line < 4) & ((tile // 4) % 4 == line)) | ((line >= 4) & (line < 8) & (tile // 16 == line - 4))
    sums = jnp.dot(need.astype(BF16), jnp.where(inside, 1.0, 0.0).astype(BF16), preferred_element_type=F32)
    chip = lax.broadcasted_iota(jnp.int32, (16, 128), 0)
    line = lax.broadcasted_iota(jnp.int32, (16, 128), 1)
    own = (line == chip % 4) | (line == chip // 4 + 4)
    most[0] = jnp.max(jnp.where(own, 0.0, sums)).astype(jnp.int32)


def make_tables(sources, counts):
    smem, vmem = pl.BlockSpec(memory_space=pltpu.SMEM), pl.BlockSpec(memory_space=pltpu.VMEM)
    return pl.pallas_call(
        tables,
        out_shape=(
            jax.ShapeDtypeStruct((3, 16), jnp.int32),
            jax.ShapeDtypeStruct((5, 16), jnp.int32),
            jax.ShapeDtypeStruct((1,), jnp.int32),
        ),
        in_specs=[smem, smem, vmem, vmem],
        out_specs=(smem, smem, smem),
        scratch_shapes=[pltpu.SMEM((3, 16), jnp.int32)],
    )(sources, counts, sources, counts.reshape(-1, 1))


def main(
    cap, width, pack_i, lad_i, a_ref, b_ref, amp_ref, l_ref, eo_ref, ev_ref,
    res_ref, new_ref, norm_ref,
    abuf, bbuf, ampbuf, lbuf, evbuf, cyc, row0, row1, row2, row3, packs, got0, got1, got2, got3,
    resbuf, newbuf, nacc, nbuf, ssem, rsem, lsem,
):
    core, p, q, x, y = place()
    z = lax.axis_index("occ")
    sister = 1 - core
    rows, got = (row0, row1, row2, row3), (got0, got1, got2, got3)
    half_k = width // 2
    relay = 3 * half_k // 2

    def at(fp, fq):
        fp, fq = fp % RING, fq % RING
        return (z, jnp.where(core == 0, (fp * 4 + fq) * 2, (fq * 4 + fp) * 2 + 1))

    def chip_core(zz, cc):
        return (zz, (x * 4 + y) * 2 + cc)

    partners = [at(p + d, q) for d in DIST] + [at(p, q + d) for d in DIST]
    group = [((z + dz) % 4, (core + dc) % 2) for dz in range(4) for dc in range(2) if dz or dc]
    partners += [chip_core(*one) for one in group]
    barrier = pltpu.get_barrier_semaphore()
    for one in partners:
        pl.semaphore_signal(barrier, inc=1, device_id=one, device_id_type=MESH)

    numbers, made = {}, {}

    def describe(key, src, dst, dev):
        n = numbers.setdefault(key, len(numbers))
        return pltpu.make_async_remote_copy(
            src_ref=src, dst_ref=dst, send_sem=ssem.at[n], recv_sem=rsem.at[n], device_id=dev, device_id_type=MESH
        )

    def send(key, src, dst, dev):
        made[key] = describe(key, src, dst, dev)
        made[key].start()

    def arrived(key):
        made[key].wait_recv()

    loads = []

    def load(src, dst):
        one = pltpu.make_async_copy(src, dst, lsem.at[len(loads)])
        one.start()
        loads.append(one)
        return one

    own_b = load(b_ref, bbuf.at[core])
    own_amp = load(amp_ref.at[core], ampbuf.at[core])
    own_l = load(l_ref, lbuf.at[core])

    for at_col in range(0, half_k, 1024):
        left = a_ref[:, at_col : at_col + 1024].astype(F32)
        right = a_ref[:, half_k + at_col : half_k + at_col + 1024].astype(F32)
        abuf[0, p, :, at_col : at_col + 1024] = left[:16].astype(BF16)
        abuf[0, p, :, half_k + at_col : half_k + at_col + 1024] = right[:16].astype(BF16)
        abuf[0, p, :, width + at_col : width + at_col + 1024] = jnp.concatenate([left[16:], right[16:]], axis=0).astype(BF16)
    evbuf[core] = ev_ref[...]

    pl.semaphore_wait(barrier, len(partners))

    firsthalf, secondhalf = pl.ds(0, relay), pl.ds(relay, relay)

    def along_first(i):
        if i == 3:
            pp = (p + 3) % RING
            send(("a1r", 3), abuf.at[0, pp, :, firsthalf], abuf.at[0, pp, :, firsthalf], at(p + 1, q))
        else:
            pp = (p + 1) % RING
            send(("a1r", 1), abuf.at[0, pp, :, secondhalf], abuf.at[0, pp, :, secondhalf], at(p - 1, q))

    def spread(i):
        pp = (p + i) % RING
        send(("a2", i, 1), abuf.at[0, pp], abuf.at[3, pp], at(p, q + 1))
        send(("a2", i, 3), abuf.at[0, pp], abuf.at[1, pp], at(p, q - 1))

    def pass_on(i):
        pp = (p + i) % RING
        arrived(("a2", i, 1))
        send(("a2r", i, 1), abuf.at[3, pp, :, firsthalf], abuf.at[2, pp, :, firsthalf], at(p, q + 1))
        arrived(("a2", i, 3))
        send(("a2r", i, 3), abuf.at[1, pp, :, secondhalf], abuf.at[2, pp, :, secondhalf], at(p, q - 1))

    send(("a1", 1), abuf.at[0, p], abuf.at[0, p], at(p + 1, q))
    send(("a1", 3), abuf.at[0, p], abuf.at[0, p], at(p - 1, q))
    spread(0)
    to_sister = chip_core(z, sister)
    send("b", b_ref, bbuf.at[core], to_sister)
    send("amp", amp_ref.at[sister], ampbuf.at[core], to_sister)
    send("l", l_ref, lbuf.at[core], to_sister)
    send("ev", ev_ref, evbuf.at[core], to_sister)

    arrived(("a1", 1))
    along_first(3)
    arrived(("a1", 3))
    along_first(1)
    spread(3)
    spread(1)
    pass_on(0)
    arrived(("a1r", 3))
    arrived(("a1r", 1))
    spread(2)

    def multiply(j):
        row = (q + j) % RING

        def one_tile(t, carry):
            cc = t // 2
            cols = pl.ds(pl.multiple_of((t % 2) * 256, 256), 256)
            low = abuf[j, :, :, 0:half_k].reshape(64, half_k)
            high = abuf[j, :, :, half_k:width].reshape(64, half_k)
            tail = abuf[j, :, :, width : width + half_k].reshape(64, half_k)
            sum0 = jnp.dot(
                jnp.concatenate([low, tail], axis=0), bbuf[cc, 0:half_k, cols], preferred_element_type=F32
            )
            sum1 = jnp.dot(
                jnp.concatenate([high, tail], axis=0), bbuf[cc, half_k:width, cols], preferred_element_type=F32
            )
            main_rows = sum0[:64] + sum1[:64]
            tail_rows = sum0[64:].reshape(4, 2, 8, 256)[:, 0] + sum1[64:].reshape(4, 2, 8, 256)[:, 1]
            cycle = jnp.concatenate([main_rows, tail_rows.reshape(32, 256)], axis=0).astype(BF16)
            cyc[j, t] = cycle
            amps = ampbuf[cc, row, :, cols].astype(F32)
            rows[j][p * 4 + t] = (amps + cycle.astype(F32)).astype(BF16)
            return carry

        lax.fori_loop(0, 4, one_tile, 0)

    def share(j):
        mine = pl.ds(p * 4, 4)
        send(("e1", j, 1), rows[j].at[mine], rows[j].at[mine], at(p + 1, q))
        send(("e1", j, 3), rows[j].at[mine], rows[j].at[mine], at(p - 1, q))

    def share_on(j):
        arrived(("e1", j, 1))
        two = pl.ds(((p + 3) % RING) * 4, 2)
        send(("e1r", j, 1), rows[j].at[two], rows[j].at[two], at(p + 1, q))
        arrived(("e1", j, 3))
        two = pl.ds(((p + 1) % RING) * 4 + 2, 2)
        send(("e1r", j, 3), rows[j].at[two], rows[j].at[two], at(p - 1, q))

    def hand_out(j):
        arrived(("e1r", j, 1))
        arrived(("e1r", j, 3))
        for g, d in enumerate(DIST):

            def one_slot(s, carry, g=g):
                packs[j, g * cap + s] = rows[j][pack_i[g, s]]
                return carry

            lax.fori_loop(0, cap, one_slot, 0)
            there = DIST.index((-d) % RING)
            send(
                ("e2", j, g), packs.at[j, pl.ds(g * cap, cap)], got[(j - d) % RING].at[pl.ds(there * cap, cap)],
                at(p, q + d),
            )

    own_b.wait()
    own_amp.wait()
    own_l.wait()
    arrived("amp")
    arrived("ev")
    arrived("l")

    def mask_weights(s, carry):
        t, k = s // 4, s % 4
        slot = (t % 2) * 4 + k
        lbuf[t // 2, slot] = lbuf[t // 2, slot] * lad_i[4, s].astype(F32).astype(BF16)
        return carry

    lax.fori_loop(0, 16, mask_weights, 0)
    pass_on(3)
    pass_on(1)
    arrived("b")
    multiply(0)
    share(0)
    pass_on(2)
    share_on(0)
    multiply(1)
    share(1)
    multiply(3)
    share(3)
    hand_out(0)
    share_on(1)
    share_on(3)
    for i in range(RING):
        arrived(("a2r", i, 1))
        arrived(("a2r", i, 3))
    multiply(2)
    share(2)
    hand_out(1)
    share_on(2)
    hand_out(3)
    hand_out(2)

    nacc[...] = jnp.zeros_like(nacc)

    def finish(j):
        for g, d in enumerate(DIST):
            arrived(("e2", (j - d) % RING, DIST.index((-d) % RING)))
        row = (q + j) % RING

        def one_tile(t, carry):
            cc = t // 2
            cols = pl.ds(pl.multiple_of((t % 2) * 256, 256), 256)
            total = jnp.zeros((96, 256), F32)
            for k in range(4):
                s = t * 4 + k
                near = rows[j][lad_i[0, s]].astype(F32)
                far = got[j][lad_i[1, s] * cap + lad_i[2, s]].astype(F32)
                block = jnp.where(lad_i[3, s] == 1, near, far).astype(BF16)
                total += jnp.dot(block, lbuf[cc, (t % 2) * 4 + k], preferred_element_type=F32)
            residual = (total + cyc[j, t].astype(F32)).astype(BF16)
            wide = residual.astype(F32)
            denom = eo_ref[row] + evbuf[cc, 0:1, cols]
            resbuf[j, cc, :, cols] = residual
            newbuf[j, cc, :, cols] = (ampbuf[cc, row, :, cols].astype(F32) - wide / denom).astype(BF16)
            nacc[...] += (wide * wide).reshape(12, 8, 256).sum(axis=0)
            return carry

        lax.fori_loop(0, 4, one_tile, 0)
        load(resbuf.at[j, core], res_ref.at[core, row])
        load(newbuf.at[j, core], new_ref.at[core, row])
        send(("res", j), resbuf.at[j, sister], res_ref.at[core, row], to_sister)
        send(("new", j), newbuf.at[j, sister], new_ref.at[core, row], to_sister)

    for j in (2, 0, 1, 3):
        finish(j)

    value = jnp.sum(nacc[...])
    line = ([(q + d) % 4 for d in DIST], q, [at(p, q + d) for d in DIST])
    ring = ([(p + d) % 4 for d in DIST], p, [at(p + d, q) for d in DIST])
    rest = (None, z * 2 + core, [chip_core(*one) for one in group])
    for stage, (_, slot, devices) in enumerate((line, ring, rest)):
        nbuf[stage, slot] = jnp.full((8, 128), value, F32)
        for n, dev in enumerate(devices):
            send(("n", stage, n), nbuf.at[stage, slot], nbuf.at[stage, slot], dev)
        for n in range(len(devices)):
            arrived(("n", stage, n))
        total = nbuf[stage, 0]
        for n in range(1, len(devices) + 1):
            total = total + nbuf[stage, n]
        if stage < 2:
            value = total
            value = jnp.max(value)
    norm_ref[...] = total

    for j in range(RING):
        arrived(("res", j))
        arrived(("new", j))
    for one in loads[3:]:
        one.wait()
    for one in made.values():
        one.wait_send()


COPIES = 80


def run_main(cap, number, pack, lad, a, b, amp, blocks, eo, ev):
    width, columns = b.shape
    rows = amp.shape[2]
    smem, vmem = pl.BlockSpec(memory_space=pltpu.SMEM), pl.BlockSpec(memory_space=pltpu.VMEM)
    anywhere = pl.BlockSpec(memory_space=pl.ANY)
    out = jax.ShapeDtypeStruct((2, RING, rows, columns), BF16)
    row_buf = pltpu.VMEM((16, rows, 256), BF16)
    got_buf = pltpu.VMEM((3 * cap, rows, 256), BF16)
    return pl.pallas_call(
        functools.partial(main, cap, width),
        out_shape=(out, out, jax.ShapeDtypeStruct((8, 128), F32)),
        in_specs=[smem, smem, vmem, anywhere, anywhere, anywhere, vmem, vmem],
        out_specs=(anywhere, anywhere, vmem),
        scratch_shapes=[
            pltpu.VMEM((RING, RING, 16, width + width // 2), BF16),
            pltpu.VMEM((2, width, columns), BF16),
            pltpu.VMEM((2, RING, rows, columns), BF16),
            pltpu.VMEM((2, 8, 256, 256), BF16),
            pltpu.VMEM((2, 8, columns), F32),
            pltpu.VMEM((RING, 4, rows, 256), BF16),
            row_buf, row_buf, row_buf, row_buf,
            pltpu.VMEM((RING, 3 * cap, rows, 256), BF16),
            got_buf, got_buf, got_buf, got_buf,
            pltpu.VMEM((RING, 2, rows, columns), BF16),
            pltpu.VMEM((RING, 2, rows, columns), BF16),
            pltpu.VMEM((8, 256), F32),
            pltpu.VMEM((3, 8, 8, 128), F32),
            pltpu.SemaphoreType.DMA((COPIES,)),
            pltpu.SemaphoreType.DMA((COPIES,)),
            pltpu.SemaphoreType.DMA((11,)),
        ],
        compiler_params=pltpu.CompilerParams(
            collective_id=number, has_side_effects=True, vmem_limit_bytes=60 * 2**20
        ),
        cost_estimate=pl.CostEstimate(flops=8 * 10**9, bytes_accessed=20 * 2**20, transcendentals=0),
    )(pack, lad, a, b, amp, blocks, eo, ev)


def to_core_rows(array):
    rest = array.shape[1:]
    blocks = array.reshape(RING, RING, 2, 24, *rest)
    swap = (1, 0) + tuple(range(2, 3 + len(rest)))
    both = jnp.stack([blocks[:, :, 0].transpose(swap), blocks[:, :, 1]])
    return jnp.concatenate(
        [both[:, :, :, :16].reshape(2, RING, 64, *rest), both[:, :, :, 16:].reshape(2, RING, 32, *rest)], axis=2
    )


def from_core_rows(array):
    rest = array.shape[3:]
    both = jnp.concatenate(
        [array[:, :, :64].reshape(2, RING, RING, 16, *rest), array[:, :, 64:].reshape(2, RING, RING, 8, *rest)], axis=3
    )
    swap = (1, 0) + tuple(range(2, 3 + len(rest)))
    return jnp.stack([both[0].transpose(swap), both[1]], axis=2).reshape(RING * RING * 2 * 24, *rest)


def on_device(amps, cycle_amps, cycle_ints, ladder_ints, sources, counts, eps_occ, eps_vir):
    core = lax.axis_index("vir") % 2
    pack, lad, most = make_tables(sources, counts)
    amp = to_core_rows(amps)
    eo = lax.dynamic_index_in_dim(to_core_rows(eps_occ), core, 0, False)[..., None]
    ev = jnp.broadcast_to(eps_vir[None, :], (8, eps_vir.shape[0]))
    blocks = ladder_ints.reshape(8, *ladder_ints.shape[2:])
    branches = [functools.partial(run_main, cap, n) for n, cap in enumerate(CAPS)]
    which = sum((most[0] > cap).astype(jnp.int32) for cap in CAPS[:-1])
    residual, new_amps, norm = lax.switch(
        which, branches, pack, lad, cycle_amps, cycle_ints, amp, blocks, eo, ev
    )
    return from_core_rows(residual), from_core_rows(new_amps), norm[0, 0]


def solution(mesh):
    placed = (
        P("occ", "vir"),
        P(("occ", "vir"), None),
        P(None, "vir"),
        P("vir", None, None, None),
        P(),
        P(),
        P("occ"),
        P("vir"),
    )
    return jax.shard_map(
        on_device,
        mesh=mesh,
        in_specs=placed,
        out_specs=(P("occ", "vir"), P("occ", "vir"), P()),
        check_vma=False,
    )
```

time: 279 us -> 121 us (0.43)
  waiting for transfers between devices: 161 us -> 0 us
  Pallas kernels: 0 us -> 107 us
  blocking collectives: 66.8 us -> 0 us
  between operations: 24.3 us -> 2.07 us
  matrix products: 21.5 us -> 0 us
  local copies, waits for them, and re-layouts: 1.44 us -> 8.78 us
    all_gather x2 -> x0, waiting for transfers between devices: 160 us -> none  [the longest x1 91.2 us: on_device(): shard_piece = lax.all_gather(dressed, 'vir', axis=1, tiled=True)]
    pallas_call x0 -> x2, Pallas kernels: none -> 107 us  [the longest x1 104 us: run_main(): pl.pallas_call(functools.partial(main, cap, width), out_shape=(out, out,...]
    psum x1 -> x0, blocking collectives: 66.8 us -> none  [on_device(): residual_norm = lax.psum(jnp.sum(res_wide * res_wide), ('occ', 'vir'))]
    dot_general x7 -> x0, matrix products: 21.5 us -> none  [the longest x1 13 us: on_device(): jnp.dot(lax.all_gather(cycle_amps, 'vir', axis=0, tiled=True), cycle_ints...]
  transfers between devices with their start and end apart: 2 -> 0, of which waited for: 2 -> 0; matrix products, arithmetic and copies ran while one was open for 1% -> 0% of each run, Pallas kernels for 0% -> 0%
where the time goes in v1:
time: 121 us
  Pallas kernels  107 us (88%)
  local copies, waits for them, and re-layouts  8.78 us (7%)
  other arithmetic  2.36 us (2%)
  between operations  2.07 us (2%)
    pallas_call x1, Pallas kernels, run_main(): pl.pallas_call(functools.partial(main, cap, width), out_shape=(out, out,...  104 us
    pallas_call x1, Pallas kernels, make_tables(): pl.pallas_call(tables, out_shape=(jax.ShapeDtypeStruct((3, 16), jnp.int32...  3.79 us
    unnamed x7, local copies, waits for them, and re-layouts  2.53 us

profile of v1, /device:TPU:1, one launch (start us, length us, event | category | flops | bytes accessed | tf_op | source)
XLA Modules:
  0.0 120.7 jit_solution(11560007630271811044)
XLA Ops:
  0.6 0.8 reshape.71
  1.5 0.1 pad_maximum_fusion.6
  1.5 0.1 reshape.73
  1.6 0.1 reshape.72
  1.7 0.1 pad_maximum_fusion.7
  1.8 1.4 %copy.22.sources.sources_v = s32[64,4]{1,0:T(8,128)} copy(s32[64,4]{0,1:T(4,128)} %param.15) | data formatting | bytes 2048 | tf_op args[4]
  3.2 1.4 %copy.24.counts_v = s32[64,1]{1,0:T(8,128)} copy(s32[64,1]{0,1:T(1,128)} %bitcast.73) | data formatting | bytes 512 | tf_op jit(solution)/shard_map/reshape | solution.py:107
  4.5 3.8 %shard_map.103 = (s32[3,16]{1,0:T(4,128)S(1)}, s32[5,16]{1,0:T(8,128)S(1)}, s32[1]{0:T(128)}) custom-call(s32[64,4]{1,0:T(8,128)} %copy.22.sources.sources_v, s32[64]{0:T(128)} %counts.1, s32[64,4]{1,0:T(8,128)} %copy.22.sources.sources_v, s32[64,1]{1,0:T(8,128)} %copy.24.counts_v), custom_call_target="tpu_custom_call" | custom-call | tf_op jit(solution)/shard_map/pallas_call | solution.py:97
  9.6 1.2 fusion.8
  10.9 0.0 copy-start
  10.9 0.0 copy-start.1
  10.9 0.1 fusion
  11.0 0.1 pad_maximum_fusion
  11.0 0.5 copy-done
  11.6 0.6 copy-done.1
  12.1 106.3 %conditional.1 = (bf16[2,4,96,512]{3,2,1,0:T(8,128)(2,1)S(1)}, bf16[2,4,96,512]{3,2,1,0:T(8,128)(2,1)S(1)}, f32[]{:T(128)}) conditional(s32[]{:T(128)} %bitcast.10, (bf16[2,4,256,256]{3,2,1,0:T(8,128)(2,1)S(1)}, s32[]{:T(128)}, f32[2,4,96]{2,1,0:T(4,128)S(1)}, f32[512]{0:T(512)S(1)}, s32[3,16]{1,0:T(4,128)S(1)}, ...), branch_computations={%region_0.1_spmd, %region_1.2_spmd, %region_2.3_spmd} | conditional | flops 8000000000 | bytes 20996166 | solution.py:438
  12.1 0.6 broadcast_in_dim.24.ev_ref
  12.8 0.8 copy.19.eo_ref
  13.6 103.6 %branch_0_fun.2 = (bf16[2,4,96,512]{3,2,1,0:T(8,128)(2,1)S(1)}, bf16[2,4,96,512]{3,2,1,0:T(8,128)(2,1)S(1)}, f32[8,128]{1,0:T(8,128)}) custom-call(s32[3,16]{1,0:T(4,128)S(1)} %get-tuple-element.175.pack_i, s32[5,16]{1,0:T(8,128)S(1)} %get-tuple-element.176.lad_i, bf16[24,8192]{1,0:T(8,128)(2,1)} %get-tuple-element.177.a_ref, ...), custom_call_target="tpu_custom_call" | custom-call | flops 8000000000 | bytes 20971520 | tf_op jit(solution)/shard_map/cond/branch_0_fun/pallas_call | solution.py:380
  117.2 1.2 slice.42
  118.6 0.1 fusion.4
  118.6 1.0 pad_maximum_fusion.1
  119.6 0.1 fusion.2
  119.7 1.0 pad_maximum_fusion.2
  (9 shorter events, 0.2 us)
Async XLA Ops:
  10.9 0.7 copy-start
  10.9 1.2 %copy-start.1 = (bf16[2,4,256,256]{3,2,1,0:T(8,128)(2,1)S(1)}, bf16[2,4,256,256]{3,2,1,0:T(8,128)(2,1)}, u32[]{:S(2)}) copy-start(bf16[2,4,256,256]{3,2,1,0:T(8,128)(2,1)} %param.14) | copy-start | bytes 3145732

commit v2 on v1

v2 whole, which is shorter than its diff:
```python
import functools

import jax
import jax.numpy as jnp
from jax import lax
from jax.experimental import pallas as pl
from jax.experimental.pallas import tpu as pltpu
from jax.sharding import PartitionSpec as P

MESH = pl.DeviceIdType.MESH
RING = 4
DIST = (1, 3, 2)
CAPS = (6, 8, 16)
ORDER = (0, 1, 3, 2)
F32, BF16 = jnp.float32, jnp.bfloat16


def place():
    vir = lax.axis_index("vir")
    core = vir % 2
    y = (vir // 2) % RING
    x = vir // (2 * RING)
    first = jnp.where(core == 0, x, y)
    second = jnp.where(core == 0, y, x)
    return core, first, second, x, y


def tables(sources, counts, plan, which):
    core, p, q, x, y = place()

    def iota(shape, axis):
        return lax.broadcasted_iota(jnp.int32, shape, axis)

    def ones(mask):
        return jnp.where(mask, 1.0, 0.0)

    def dot(one, other):
        return jnp.dot(one.astype(BF16), other.astype(BF16), preferred_element_type=F32)

    def split(tile):
        tx, ty = tile // 16, (tile // 4) % 4
        return jnp.where(core == 0, tx, ty), jnp.where(core == 0, ty, tx), tile % 4

    tile = iota((64, 64), 0)
    hits = jnp.zeros((64, 64), F32)
    for k in range(4):
        hits += ones((sources[k : k + 1, :] == tile) & (counts[...] > k))
    need = jnp.minimum(dot(hits, ones(iota((64, 128), 0) // 4 == iota((64, 128), 1))), 1.0)

    line, member = iota((16, 64), 0), iota((16, 64), 1)
    inside = ((line < 4) & ((member // 4) % 4 == line)) | ((line >= 4) & (line < 8) & (member // 16 == line - 4))
    line, chip = iota((16, 128), 0), iota((16, 128), 1)
    own = ((line < 4) & (chip % 4 == line)) | (chip // 4 + 4 == line)
    most = jnp.max(jnp.where(own, 0.0, dot(ones(inside), need))).astype(jnp.int32)
    branch, cap = jnp.int32(0), jnp.int32(CAPS[0])
    for n, limit in enumerate(CAPS[:-1]):
        branch = jnp.where(most > limit, n + 1, branch)
        cap = jnp.where(most > limit, CAPS[n + 1], cap)
    which[0] = branch

    tp, tq, tt = split(tile)
    op, oq, ot = split(iota((64, 64), 1))
    placed = dot(ones((tq == oq) & (op * 4 + ot < tp * 4 + tt)), need)
    sp, sq, st = split(iota((64, 1), 0))
    entry = (sp * 4 + st).astype(F32)
    chip, slot = iota((64, 128), 1), iota((64, 128), 1).astype(F32)
    plan[...] = jnp.zeros_like(plan)
    for g, d in enumerate(DIST):
        other = (q + d) % RING
        there = chip == jnp.where(core == 0, p * 4 + other, other * 4 + p)
        wants = jnp.sum(jnp.where(there, need, 0.0), axis=1, keepdims=True)
        where = jnp.sum(jnp.where(there, placed, 0.0), axis=1, keepdims=True)
        taken = (wants > 0.0) & (sq == q) & (where == slot)
        plan[g : g + 1, :] = jnp.sum(jnp.where(taken, entry, 0.0), axis=0, keepdims=True).astype(jnp.int32)
    where = jnp.sum(jnp.where(chip == x * 4 + y, placed, 0.0), axis=1, keepdims=True)
    for k in range(4):
        source = sources[k : k + 1, :]
        tp, tq, tt = split(source)
        after = jnp.sum(jnp.where(source == tile, where, 0.0), axis=0, keepdims=True).astype(jnp.int32)
        live = counts[...] > k
        near = tq == q
        d = (tq - q + RING) % RING
        group = jnp.where(d == 1, 0, jnp.where(d == 3, 1, 2))
        plan[4 + k : 5 + k, 0:64] = jnp.where(live & near, tp * 4 + tt, p * 4)
        plan[8 + k : 9 + k, 0:64] = jnp.where(live & ~near, group * cap + after, 0)
        plan[12 + k : 13 + k, 0:64] = jnp.where(live & ~near, 0, 1)
        plan[16 + k : 17 + k, 0:64] = jnp.where(live, 1, 0)


def make_tables(sources, counts):
    smem, vmem = pl.BlockSpec(memory_space=pltpu.SMEM), pl.BlockSpec(memory_space=pltpu.VMEM)
    return pl.pallas_call(
        tables,
        out_shape=(jax.ShapeDtypeStruct((24, 128), jnp.int32), jax.ShapeDtypeStruct((1,), jnp.int32)),
        in_specs=[vmem, vmem],
        out_specs=(vmem, smem),
    )(sources.T, counts.reshape(1, -1))


def main(
    cap, width, plan, a_ref, b_ref, amp_ref, l_ref, eo_ref, ev_ref,
    res_ref, new_ref, norm_ref,
    abuf, bbuf, amps_mine, amps_away, ampbuf, lbuf, occ, cyc, row0, row1, row2, row3, packs, got0, got1, got2, got3,
    resbuf, resin, nacc, nbuf, ssem, rsem, lsem,
):
    core, p, q, x, y = place()
    z = lax.axis_index("occ")
    sister = 1 - core
    rows, got = (row0, row1, row2, row3), (got0, got1, got2, got3)
    half_k = width // 2
    relay = 3 * half_k // 2

    def at(fp, fq):
        fp, fq = fp % RING, fq % RING
        return (z, jnp.where(core == 0, (fp * 4 + fq) * 2, (fq * 4 + fp) * 2 + 1))

    def on_chip(zz, cc):
        return (zz, (x * 4 + y) * 2 + cc)

    group = [on_chip((z + dz) % 4, (core + dc) % 2) for dz in (2, 1, 3, 0) for dc in (1, 0) if dz or dc]
    plane = [at(p + dp, q + dq) for dp in (2, 1, 3, 0) for dq in (2, 1, 3, 0) if dp or dq]
    partners = group + plane
    barrier = pltpu.get_barrier_semaphore()
    for one in partners:
        pl.semaphore_signal(barrier, inc=1, device_id=one, device_id_type=MESH)

    made = {}

    def send(key, src, dst, dev):
        n = len(made)
        made[key] = pltpu.make_async_remote_copy(
            src_ref=src, dst_ref=dst, send_sem=ssem.at[n], recv_sem=rsem.at[n], device_id=dev, device_id_type=MESH
        )
        made[key].start()

    def arrived(key):
        made[key].wait_recv()

    own_b = pltpu.make_async_copy(b_ref, bbuf.at[core], lsem.at[0])
    own_l = pltpu.make_async_copy(l_ref, lbuf.at[core], lsem.at[1])
    own_b.start()
    own_l.start()

    for at_col in range(0, half_k, 1024):
        left = a_ref[:, at_col : at_col + 1024].astype(F32)
        right = a_ref[:, half_k + at_col : half_k + at_col + 1024].astype(F32)
        abuf[0, p, :, at_col : at_col + 1024] = left[:16].astype(BF16)
        abuf[0, p, :, half_k + at_col : half_k + at_col + 1024] = right[:16].astype(BF16)
        abuf[0, p, :, width + at_col : width + at_col + 1024] = jnp.concatenate([left[16:], right[16:]], axis=0).astype(BF16)

    pl.semaphore_wait(barrier, len(partners))

    halves = (pl.ds(0, relay), pl.ds(relay, relay))

    def along_first(way, h):
        send(("a1", way, h), abuf.at[0, p, :, halves[h]], abuf.at[0, p, :, halves[h]], at(p + way, q))

    def spread(i):
        pp = (p + i) % RING
        for n in range(2):
            send(("a2", i, 1, n), abuf.at[0, pp, :, halves[n]], abuf.at[3, pp, :, halves[n]], at(p, q + 1))
            m = 1 - n
            send(("a2", i, -1, m), abuf.at[0, pp, :, halves[m]], abuf.at[1, pp, :, halves[m]], at(p, q - 1))

    def pass_on(i):
        pp = (p + i) % RING
        arrived(("a2", i, 1, 0))
        send(("a2r", i, 1), abuf.at[3, pp, :, halves[0]], abuf.at[2, pp, :, halves[0]], at(p, q + 1))
        arrived(("a2", i, -1, 1))
        send(("a2r", i, -1), abuf.at[1, pp, :, halves[1]], abuf.at[2, pp, :, halves[1]], at(p, q - 1))

    along_first(1, 0)
    along_first(-1, 1)
    along_first(1, 1)
    along_first(-1, 0)
    to_sister = on_chip(z, sister)
    send("b", b_ref, bbuf.at[core], to_sister)
    send("l", l_ref, lbuf.at[core], to_sister)

    def amps_of(cc, keep):
        for fq in range(RING):
            for pair in range(0, RING, 2):
                tails = []
                for fp in (pair, pair + 1):
                    chip = fp * 4 + fq if cc == 0 else fq * 4 + fp
                    block = amp_ref[48 * chip : 48 * chip + 48, :].astype(F32)
                    block = block[24 * cc : 24 * cc + 24]
                    keep[fq, 16 * fp : 16 * fp + 16, :] = block[:16].astype(BF16)
                    tails.append(block[16:])
                keep[fq, 64 + 8 * pair : 80 + 8 * pair, :] = jnp.concatenate(tails, axis=0).astype(BF16)

    @pl.when(core == 0)
    def _():
        amps_of(0, amps_mine)
        amps_of(1, amps_away)

    @pl.when(core == 1)
    def _():
        amps_of(1, amps_mine)
        amps_of(0, amps_away)

    send("amp", amps_away, ampbuf, to_sister)

    pp, pm = (p + 1) % RING, (p + 3) % RING
    arrived(("a1", 1, 0))
    send(("a1r", 1), abuf.at[0, pm, :, halves[0]], abuf.at[0, pm, :, halves[0]], at(p + 1, q))
    arrived(("a1", -1, 1))
    send(("a1r", -1), abuf.at[0, pp, :, halves[1]], abuf.at[0, pp, :, halves[1]], at(p - 1, q))
    spread(0)
    for part in range(eo_ref.shape[1] // 128):
        values = jnp.broadcast_to(eo_ref[:, part * 128 : part * 128 + 128], (128, 128))
        occ[part * 128 : part * 128 + 128, :] = values.T
    arrived(("a1", 1, 1))
    spread(3)
    arrived(("a1", -1, 0))
    spread(1)
    arrived(("a1r", 1))
    arrived(("a1r", -1))
    spread(2)

    def multiply(j, first, tiles):
        row = (q + j) % RING

        def one_tile(n, carry):
            cc = (core + n // 2) % 2
            t = cc * 2 + n % 2
            cols = pl.ds(pl.multiple_of((t % 2) * 256, 256), 256)
            low = abuf[j, :, :, 0:half_k].reshape(64, half_k)
            high = abuf[j, :, :, half_k:width].reshape(64, half_k)
            tail = abuf[j, :, :, width : width + half_k].reshape(64, half_k)
            sum0 = jnp.dot(
                jnp.concatenate([low, tail], axis=0), bbuf[cc, 0:half_k, cols], preferred_element_type=F32
            )
            sum1 = jnp.dot(
                jnp.concatenate([high, tail], axis=0), bbuf[cc, half_k:width, cols], preferred_element_type=F32
            )
            main_rows = sum0[:64] + sum1[:64]
            tail_rows = sum0[64:].reshape(4, 2, 8, 256)[:, 0] + sum1[64:].reshape(4, 2, 8, 256)[:, 1]
            cycle = jnp.concatenate([main_rows, tail_rows.reshape(32, 256)], axis=0).astype(BF16)
            cyc[j, t] = cycle
            amps = jnp.where(cc == core, amps_mine[row, :, cols].astype(F32), ampbuf[row, :, cols].astype(F32))
            rows[j][p * 4 + t] = (amps + cycle.astype(F32)).astype(BF16)
            return carry

        lax.fori_loop(first, first + tiles, one_tile, 0)

    def share(j):
        mine = pl.ds(p * 4, 4)
        send(("e1", j, 1), rows[j].at[mine], rows[j].at[mine], at(p + 1, q))
        send(("e1", j, -1), rows[j].at[mine], rows[j].at[mine], at(p - 1, q))

    def share_on(j):
        arrived(("e1", j, 1))
        two = pl.ds(pm * 4, 2)
        send(("e1r", j, 1), rows[j].at[two], rows[j].at[two], at(p + 1, q))
        arrived(("e1", j, -1))
        two = pl.ds(pp * 4 + 2, 2)
        send(("e1r", j, -1), rows[j].at[two], rows[j].at[two], at(p - 1, q))

    def hand_out(j):
        arrived(("e1r", j, 1))
        arrived(("e1r", j, -1))
        for g in (2, 0, 1):
            d = DIST[g]

            def one_slot(s, carry, g=g):
                packs[j, g * cap + s] = rows[j][plan[g, s]]
                return carry

            lax.fori_loop(0, cap, one_slot, 0)
            there = DIST.index((-d) % RING)
            send(
                ("e2", j, g), packs.at[j, pl.ds(g * cap, cap)], got[(j - d) % RING].at[pl.ds(there * cap, cap)],
                at(p, q + d),
            )

    pass_on(0)
    own_b.wait()
    arrived("amp")
    multiply(0, 0, 2)
    pass_on(3)
    arrived("b")
    multiply(0, 2, 2)
    share(0)
    pass_on(1)
    own_l.wait()
    arrived("l")
    mine = (x * 4 + y) * 4

    def mask_weights(s, carry):
        t, k = s // 4, s % 4
        slot = (t % 2) * 4 + k
        lbuf[t // 2, slot] = lbuf[t // 2, slot] * plan[16 + k, mine + t].astype(F32).astype(BF16)
        return carry

    lax.fori_loop(0, 16, mask_weights, 0)
    share_on(0)
    pass_on(2)
    for i in range(RING):
        arrived(("a2", i, 1, 1))
    multiply(3, 0, 4)
    share(3)
    for i in range(RING):
        arrived(("a2", i, -1, 0))
    hand_out(0)
    multiply(1, 0, 4)
    share(1)
    share_on(3)
    for i in range(RING):
        arrived(("a2r", i, 1))
        arrived(("a2r", i, -1))
    hand_out(3)
    multiply(2, 0, 4)
    share(2)
    share_on(1)
    hand_out(1)
    share_on(2)
    hand_out(2)

    nacc[...] = jnp.zeros_like(nacc)

    def finish(j):
        for g, d in enumerate(DIST):
            arrived(("e2", (j - d) % RING, DIST.index((-d) % RING)))
        row = (q + j) % RING

        def one_tile(t, carry):
            cols = pl.ds(pl.multiple_of((t % 2) * 256, 256), 256)
            total = jnp.zeros((96, 256), F32)
            for k in range(4):
                near = rows[j][plan[4 + k, mine + t]].astype(F32)
                far = got[j][plan[8 + k, mine + t]].astype(F32)
                block = jnp.where(plan[12 + k, mine + t] == 1, near, far).astype(BF16)
                total += jnp.dot(block, lbuf[t // 2, (t % 2) * 4 + k], preferred_element_type=F32)
            residual = (total + cyc[j, t].astype(F32)).astype(BF16)
            wide = residual.astype(F32)
            resbuf[t // 2, row, :, cols] = residual
            nacc[...] += (wide * wide).reshape(12, 8, 256).sum(axis=0)
            return carry

        lax.fori_loop(0, 4, one_tile, 0)
        send(("res", j), resbuf.at[sister, row], resin.at[row], to_sister)

    for j in (2, 0, 3, 1):
        finish(j)

    def write(first, last):
        def rows_of(cc, fq, fp):
            pair = 64 + 16 * (fp // 2)
            head = jnp.where(core == cc, resbuf[cc, fq, 16 * fp : 16 * fp + 16, :].astype(F32), resin[fq, 16 * fp : 16 * fp + 16, :].astype(F32))
            tail = jnp.where(core == cc, resbuf[cc, fq, pair : pair + 16, :].astype(F32), resin[fq, pair : pair + 16, :].astype(F32))
            return [head, tail[8 * (fp % 2) : 8 * (fp % 2) + 8]]

        for chip in range(first, last):
            fx, fy = chip // 4, chip % 4
            block = jnp.concatenate(rows_of(0, fy, fx) + rows_of(1, fx, fy), axis=0)
            here = slice(48 * chip, 48 * chip + 48)
            lanes = occ[here, :]
            denom = jnp.concatenate([lanes] * (block.shape[1] // 128), axis=1) + ev_ref[...]
            res_ref[here, :] = block.astype(BF16)
            new_ref[here, :] = (amp_ref[here, :].astype(F32) - block / denom).astype(BF16)

    def spread_norm(stage, slot, value, devices):
        nbuf[stage, slot] = jnp.full((8, 128), value, F32)
        for n, dev in enumerate(devices):
            send(("n", stage, n), nbuf.at[stage, slot], nbuf.at[stage, slot], dev)

    def sum_norm(stage, devices):
        for n in range(len(devices)):
            arrived(("n", stage, n))
        total = nbuf[stage, 0]
        for n in range(1, len(devices) + 1):
            total = total + nbuf[stage, n]
        return jnp.max(total)

    spread_norm(0, z * 2 + core, jnp.sum(nacc[...]), group)
    for j in range(RING):
        arrived(("res", j))
    write(0, 8)
    spread_norm(1, p * 4 + q, sum_norm(0, group), plane)
    write(8, 16)
    norm_ref[0] = sum_norm(1, plane)
    for one in made.values():
        one.wait_send()


COPIES = 96


def run_main(cap, number, plan, a, b, amp, blocks, eo, ev):
    width, columns = b.shape
    rows = amp.shape[0] // 8
    smem, vmem = pl.BlockSpec(memory_space=pltpu.SMEM), pl.BlockSpec(memory_space=pltpu.VMEM)
    anywhere = pl.BlockSpec(memory_space=pl.ANY)
    out = jax.ShapeDtypeStruct(amp.shape, BF16)
    row_buf = pltpu.VMEM((16, rows, 256), BF16)
    got_buf = pltpu.VMEM((3 * cap, rows, 256), BF16)
    part = pltpu.VMEM((RING, rows, columns), BF16)
    return pl.pallas_call(
        functools.partial(main, cap, width),
        out_shape=(out, out, jax.ShapeDtypeStruct((1,), F32)),
        in_specs=[smem, vmem, anywhere, vmem, anywhere, vmem, vmem],
        out_specs=(vmem, vmem, smem),
        scratch_shapes=[
            pltpu.VMEM((RING, RING, 16, width + width // 2), BF16),
            pltpu.VMEM((2, width, columns), BF16),
            part, part, part,
            pltpu.VMEM((2, 8, 256, 256), BF16),
            pltpu.VMEM((amp.shape[0], 128), F32),
            pltpu.VMEM((RING, 4, rows, 256), BF16),
            row_buf, row_buf, row_buf, row_buf,
            pltpu.VMEM((RING, 3 * cap, rows, 256), BF16),
            got_buf, got_buf, got_buf, got_buf,
            pltpu.VMEM((2, RING, rows, columns), BF16),
            part,
            pltpu.VMEM((8, 256), F32),
            pltpu.VMEM((2, 16, 8, 128), F32),
            pltpu.SemaphoreType.DMA((COPIES,)),
            pltpu.SemaphoreType.DMA((COPIES,)),
            pltpu.SemaphoreType.DMA((2,)),
        ],
        compiler_params=pltpu.CompilerParams(
            collective_id=number, has_side_effects=True, vmem_limit_bytes=60 * 2**20
        ),
        cost_estimate=pl.CostEstimate(flops=8 * 10**9, bytes_accessed=20 * 2**20, transcendentals=0),
    )(plan, a, b, amp, blocks, eo, ev)


def on_device(amps, cycle_amps, cycle_ints, ladder_ints, sources, counts, eps_occ, eps_vir):
    plan, which = make_tables(sources, counts)
    blocks = ladder_ints.reshape(8, *ladder_ints.shape[2:])
    branches = [functools.partial(run_main, cap, n) for n, cap in enumerate(CAPS)]
    residual, new_amps, norm = lax.switch(
        which[0], branches, plan, cycle_amps, cycle_ints, amps, blocks, eps_occ.reshape(1, -1), eps_vir.reshape(1, -1)
    )
    return residual, new_amps, norm[0]


def solution(mesh):
    placed = (
        P("occ", "vir"),
        P(("occ", "vir"), None),
        P(None, "vir"),
        P("vir", None, None, None),
        P(),
        P(),
        P("occ"),
        P("vir"),
    )
    return jax.shard_map(
        on_device,
        mesh=mesh,
        in_specs=placed,
        out_specs=(P("occ", "vir"), P("occ", "vir"), P()),
        check_vma=False,
    )
```

time: 121 us -> 114 us (0.942)
  local copies, waits for them, and re-layouts: 8.78 us -> 2.45 us
  other arithmetic: 2.36 us -> 0 us
    slice x5 -> x0, local copies, waits for them, and re-layouts: 2.48 us -> none  [the longest x2 1.2 us: to_core_rows(): both = jnp.stack([blocks[:, :, 0].transpose(swap), blocks[:, :, 1]])]
    pallas_call x1, Pallas kernels: 104 us -> 106 us  [run_main(): pl.pallas_call(functools.partial(main, cap, width), out_shape=(out, out,...]
    another operation x7 -> x0, other arithmetic: 2.21 us -> none  [the longest x4 2.08 us: from_core_rows(): jnp.stack([both[0].transpose(swap), both[1]], axis=2)]
    pallas_call x1, Pallas kernels: 3.79 us -> 1.6 us  [make_tables(): pl.pallas_call(tables, out_shape=(jax.ShapeDtypeStruct((24, 128), jnp.int...]
    reshape x5 -> x1, local copies, waits for them, and re-layouts: 2.35 us -> 0.69 us  [on_device(): eps_occ.reshape(1, -1)]
    broadcast_in_dim x3 -> x0, local copies, waits for them, and re-layouts: 1.42 us -> none  [the longest x2 0.82 us: on_device(): lax.dynamic_index_in_dim(to_core_rows(eps_occ), core, 0, False)[..., None]]
    unnamed x7 -> x2, local copies, waits for them, and re-layouts: 2.53 us -> 1.76 us
where the time goes in v2:
time: 114 us
  Pallas kernels  108 us (95%)
  between operations  2.99 us (3%)
  local copies, waits for them, and re-layouts  2.45 us (2%)
    pallas_call x1, Pallas kernels, run_main(): pl.pallas_call(functools.partial(main, cap, width), out_shape=(out, out,...  106 us

profile of v2, /device:TPU:1, one launch (start us, length us, event | category | flops | bytes accessed | tf_op | source)
XLA Modules:
  0.0 113.6 jit_solution(10701075394321784719)
XLA Ops:
  0.6 0.7 reshape.23
  1.3 1.6 %shard_map.106 = (s32[24,128]{1,0:T(8,128)S(1)}, s32[1]{0:T(128)}) custom-call(s32[4,64]{1,0:T(4,128)} %bitcast.8, s32[1,64]{1,0:T(1,128)} %bitcast.9), custom_call_target="tpu_custom_call" | custom-call | tf_op jit(solution)/shard_map/pallas_call | solution.py:92
  3.6 106.6 %conditional.1 = (bf16[768,512]{1,0:T(8,128)(2,1)S(1)}, bf16[768,512]{1,0:T(8,128)(2,1)S(1)}, f32[]{:T(128)}) conditional(s32[]{:T(128)} %bitcast.5, (s32[24,128]{1,0:T(8,128)S(1)}, bf16[24,8192]{1,0:T(8,128)(2,1)}, bf16[8192,512]{1,0:T(8,128)(2,1)}, bf16[768,512]{1,0:T(8,128)(2,1)}, bf16[8,256,256]{2,1,0:T(8,128)(2,1)}, ...), branch_computations={%region_0.0_spmd, %region_1.0_spmd, %region_2.0_spmd} | conditional | flops 8000000000 | bytes 20971544 | solution.py:433
  3.6 106.1 %branch_1_fun.1 = (bf16[768,512]{1,0:T(8,128)(2,1)S(1)}, bf16[768,512]{1,0:T(8,128)(2,1)S(1)}, f32[1]{0:T(128)}) custom-call(s32[24,128]{1,0:T(8,128)S(1)} %get-tuple-element.62.plan, bf16[24,8192]{1,0:T(8,128)(2,1)} %get-tuple-element.63.a_ref, bf16[8192,512]{1,0:T(8,128)(2,1)} %get-tuple-element.64.b_ref, bf16[768,512]{1,0:T(8,128)(2,1)} %get-tuple-element.65.amp_ref, ...), custom_call_target="tpu_custom_call" | custom-call | flops 8000000000 | bytes 20971520 | tf_op jit(solution)/shard_map/cond/branch_1_fun/pallas_call | solution.py:399
  110.2 0.9 copy.26
  111.0 0.9 copy.27

commit v3 on v2

--- a/solution.py
+++ b/solution.py
@@ -10,8 +10,8 @@
 MESH = pl.DeviceIdType.MESH
 RING = 4
 DIST = (1, 3, 2)
-CAPS = (6, 8, 16)
-ORDER = (0, 1, 3, 2)
+CAPS = ((6, 5), (6, 6), (8, 8), (16, 16))
+PART = 2048
 F32, BF16 = jnp.float32, jnp.bfloat16
 
 
@@ -50,12 +50,17 @@
     line, member = iota((16, 64), 0), iota((16, 64), 1)
     inside = ((line < 4) & ((member // 4) % 4 == line)) | ((line >= 4) & (line < 8) & (member // 16 == line - 4))
     line, chip = iota((16, 128), 0), iota((16, 128), 1)
-    own = ((line < 4) & (chip % 4 == line)) | (chip // 4 + 4 == line)
-    most = jnp.max(jnp.where(own, 0.0, dot(ones(inside), need))).astype(jnp.int32)
-    branch, cap = jnp.int32(0), jnp.int32(CAPS[0])
-    for n, limit in enumerate(CAPS[:-1]):
-        branch = jnp.where(most > limit, n + 1, branch)
-        cap = jnp.where(most > limit, CAPS[n + 1], cap)
+    sums = dot(ones(inside), need)
+    away = jnp.where(line < 4, line - chip % 4, line - 4 - chip // 4)
+    next_line = (away == 1) | (away == -1) | (away == 3) | (away == -3)
+    far_line = (away == 2) | (away == -2)
+    most = jnp.max(jnp.where(next_line, sums, 0.0)).astype(jnp.int32)
+    most_far = jnp.max(jnp.where(far_line, sums, 0.0)).astype(jnp.int32)
+    branch, cap = jnp.int32(len(CAPS) - 1), jnp.int32(CAPS[-1][0])
+    for n in range(len(CAPS) - 2, -1, -1):
+        enough = (most <= CAPS[n][0]) & (most_far <= CAPS[n][1])
+        branch = jnp.where(enough, n, branch)
+        cap = jnp.where(enough, CAPS[n][0], cap)
     which[0] = branch
 
     tp, tq, tt = split(tile)
@@ -98,7 +103,7 @@
 
 
 def main(
-    cap, width, plan, a_ref, b_ref, amp_ref, l_ref, eo_ref, ev_ref,
+    caps, width, plan, a_ref, b_ref, amp_ref, l_ref, eo_ref, ev_ref,
     res_ref, new_ref, norm_ref,
     abuf, bbuf, amps_mine, amps_away, ampbuf, lbuf, occ, cyc, row0, row1, row2, row3, packs, got0, got1, got2, got3,
     resbuf, resin, nacc, nbuf, ssem, rsem, lsem,
@@ -109,6 +114,8 @@
     rows, got = (row0, row1, row2, row3), (got0, got1, got2, got3)
     half_k = width // 2
     relay = 3 * half_k // 2
+    sizes = (caps[0], caps[0], caps[1])
+    bases = (0, caps[0], 2 * caps[0])
 
     def at(fp, fq):
         fp, fq = fp % RING, fq % RING
@@ -207,8 +214,8 @@
     arrived(("a1", -1, 1))
     send(("a1r", -1), abuf.at[0, pp, :, halves[1]], abuf.at[0, pp, :, halves[1]], at(p - 1, q))
     spread(0)
-    for part in range(eo_ref.shape[1] // 128):
-        values = jnp.broadcast_to(eo_ref[:, part * 128 : part * 128 + 128], (128, 128))
+    for part in range(eo_ref.shape[0] // 128):
+        values = jnp.broadcast_to(eo_ref[part * 128 : part * 128 + 128].reshape(1, 128), (128, 128))
         occ[part * 128 : part * 128 + 128, :] = values.T
     arrived(("a1", 1, 1))
     spread(3)
@@ -225,15 +232,23 @@
             cc = (core + n // 2) % 2
             t = cc * 2 + n % 2
             cols = pl.ds(pl.multiple_of((t % 2) * 256, 256), 256)
-            low = abuf[j, :, :, 0:half_k].reshape(64, half_k)
-            high = abuf[j, :, :, half_k:width].reshape(64, half_k)
-            tail = abuf[j, :, :, width : width + half_k].reshape(64, half_k)
-            sum0 = jnp.dot(
-                jnp.concatenate([low, tail], axis=0), bbuf[cc, 0:half_k, cols], preferred_element_type=F32
-            )
-            sum1 = jnp.dot(
-                jnp.concatenate([high, tail], axis=0), bbuf[cc, half_k:width, cols], preferred_element_type=F32
-            )
+
+            def one_part(n, sums):
+                start = pl.multiple_of(n * PART, PART)
+
+                def block(first):
+                    return abuf[j, :, :, pl.ds(first + start, PART)].reshape(64, PART)
+
+                def product(first):
+                    return jnp.dot(
+                        jnp.concatenate([block(first), block(width)], axis=0), bbuf[cc, pl.ds(first + start, PART), cols],
+                        preferred_element_type=F32,
+                    )
+
+                return sums[0] + product(0), sums[1] + product(half_k)
+
+            zero = jnp.zeros((128, 256), F32)
+            sum0, sum1 = lax.fori_loop(0, half_k // PART, one_part, (zero, zero))
             main_rows = sum0[:64] + sum1[:64]
             tail_rows = sum0[64:].reshape(4, 2, 8, 256)[:, 0] + sum1[64:].reshape(4, 2, 8, 256)[:, 1]
             cycle = jnp.concatenate([main_rows, tail_rows.reshape(32, 256)], axis=0).astype(BF16)
@@ -244,44 +259,43 @@
 
         lax.fori_loop(first, first + tiles, one_tile, 0)
 
-    def share(j):
-        mine = pl.ds(p * 4, 4)
-        send(("e1", j, 1), rows[j].at[mine], rows[j].at[mine], at(p + 1, q))
-        send(("e1", j, -1), rows[j].at[mine], rows[j].at[mine], at(p - 1, q))
+    def share(j, n):
+        two = pl.ds(p * 4 + 2 * ((core + n) % 2), 2)
+        for way in (1, -1):
+            send(("e1", j, way, n), rows[j].at[two], rows[j].at[two], at(p + way, q))
 
     def share_on(j):
-        arrived(("e1", j, 1))
-        two = pl.ds(pm * 4, 2)
-        send(("e1r", j, 1), rows[j].at[two], rows[j].at[two], at(p + 1, q))
-        arrived(("e1", j, -1))
-        two = pl.ds(pp * 4 + 2, 2)
-        send(("e1r", j, -1), rows[j].at[two], rows[j].at[two], at(p - 1, q))
+        for n, way, source in ((0, 1, pm), (1, -1, pp)):
+            arrived(("e1", j, way, n))
+            two = pl.ds(source * 4 + 2 * ((core + n) % 2), 2)
+            send(("e1r", j, n), rows[j].at[two], rows[j].at[two], at(p + way, q))
 
     def hand_out(j):
+        arrived(("e1", j, 1, 1))
+        arrived(("e1", j, -1, 0))
+        arrived(("e1r", j, 0))
         arrived(("e1r", j, 1))
-        arrived(("e1r", j, -1))
         for g in (2, 0, 1):
             d = DIST[g]
 
             def one_slot(s, carry, g=g):
-                packs[j, g * cap + s] = rows[j][plan[g, s]]
+                packs[j, bases[g] + s] = rows[j][plan[g, s]]
                 return carry
 
-            lax.fori_loop(0, cap, one_slot, 0)
+            lax.fori_loop(0, sizes[g], one_slot, 0)
             there = DIST.index((-d) % RING)
             send(
-                ("e2", j, g), packs.at[j, pl.ds(g * cap, cap)], got[(j - d) % RING].at[pl.ds(there * cap, cap)],
-                at(p, q + d),
+                ("e2", j, g), packs.at[j, pl.ds(bases[g], sizes[g])],
+                got[(j - d) % RING].at[pl.ds(bases[there], sizes[there])], at(p, q + d),
             )
 
     pass_on(0)
     own_b.wait()
     arrived("amp")
-    multiply(0, 0, 2)
+    multiply(0,0,2)
     pass_on(3)
     arrived("b")
-    multiply(0, 2, 2)
-    share(0)
+    multiply(0,2,2)
     pass_on(1)
     own_l.wait()
     arrived("l")
@@ -294,25 +308,31 @@
         return carry
 
     lax.fori_loop(0, 16, mask_weights, 0)
-    share_on(0)
     pass_on(2)
+    share(0, 0)
+    share(0, 1)
     for i in range(RING):
         arrived(("a2", i, 1, 1))
-    multiply(3, 0, 4)
-    share(3)
+    multiply(3,0,4)
+    share(3, 0)
+    share(3, 1)
+    share_on(0)
     for i in range(RING):
         arrived(("a2", i, -1, 0))
-    hand_out(0)
-    multiply(1, 0, 4)
-    share(1)
+    multiply(1,0,4)
+    share(1, 0)
+    share(1, 1)
     share_on(3)
+    share_on(1)
     for i in range(RING):
         arrived(("a2r", i, 1))
         arrived(("a2r", i, -1))
+    hand_out(0)
+    multiply(2,0,2)
+    share(2,0)
+    multiply(2,2,2)
+    share(2,1)
     hand_out(3)
-    multiply(2, 0, 4)
-    share(2)
-    share_on(1)
     hand_out(1)
     share_on(2)
     hand_out(2)
@@ -387,17 +407,17 @@
 COPIES = 96
 
 
-def run_main(cap, number, plan, a, b, amp, blocks, eo, ev):
+def run_main(caps, number, plan, a, b, amp, blocks, eo, ev):
     width, columns = b.shape
     rows = amp.shape[0] // 8
     smem, vmem = pl.BlockSpec(memory_space=pltpu.SMEM), pl.BlockSpec(memory_space=pltpu.VMEM)
     anywhere = pl.BlockSpec(memory_space=pl.ANY)
     out = jax.ShapeDtypeStruct(amp.shape, BF16)
     row_buf = pltpu.VMEM((16, rows, 256), BF16)
-    got_buf = pltpu.VMEM((3 * cap, rows, 256), BF16)
+    got_buf = pltpu.VMEM((2 * caps[0] + caps[1], rows, 256), BF16)
     part = pltpu.VMEM((RING, rows, columns), BF16)
     return pl.pallas_call(
-        functools.partial(main, cap, width),
+        functools.partial(main, caps, width),
         out_shape=(out, out, jax.ShapeDtypeStruct((1,), F32)),
         in_specs=[smem, vmem, anywhere, vmem, anywhere, vmem, vmem],
         out_specs=(vmem, vmem, smem),
@@ -409,7 +429,7 @@
             pltpu.VMEM((amp.shape[0], 128), F32),
             pltpu.VMEM((RING, 4, rows, 256), BF16),
             row_buf, row_buf, row_buf, row_buf,
-            pltpu.VMEM((RING, 3 * cap, rows, 256), BF16),
+            pltpu.VMEM((RING, 2 * caps[0] + caps[1], rows, 256), BF16),
             got_buf, got_buf, got_buf, got_buf,
             pltpu.VMEM((2, RING, rows, columns), BF16),
             part,
@@ -429,9 +449,9 @@
 def on_device(amps, cycle_amps, cycle_ints, ladder_ints, sources, counts, eps_occ, eps_vir):
     plan, which = make_tables(sources, counts)
     blocks = ladder_ints.reshape(8, *ladder_ints.shape[2:])
-    branches = [functools.partial(run_main, cap, n) for n, cap in enumerate(CAPS)]
+    branches = [functools.partial(run_main, caps, n) for n, caps in enumerate(CAPS)]
     residual, new_amps, norm = lax.switch(
-        which[0], branches, plan, cycle_amps, cycle_ints, amps, blocks, eps_occ.reshape(1, -1), eps_vir.reshape(1, -1)
+        which[0], branches, plan, cycle_amps, cycle_ints, amps, blocks, eps_occ, eps_vir.reshape(1, -1)
     )
     return residual, new_amps, norm[0]
 

time: 114 us -> 101 us (0.89)
  Pallas kernels: 108 us -> 95.6 us
    pallas_call x1, Pallas kernels: 106 us -> 94 us  [run_main(): pl.pallas_call(functools.partial(main, caps, width), out_shape=(out, out,...]
where the time goes in v3:
time: 101 us
  Pallas kernels  95.6 us (95%)
  between operations  3.05 us (3%)
  local copies, waits for them, and re-layouts  1.76 us (2%)
    pallas_call x1, Pallas kernels, run_main(): pl.pallas_call(functools.partial(main, caps, width), out_shape=(out, out,...  94 us

profile of v3, /device:TPU:1, one launch (start us, length us, event | category | flops | bytes accessed | tf_op | source)
XLA Modules:
  0.0 100.7 jit_solution(2747416457528022256)
XLA Ops:
  0.6 1.6 %shard_map.107 = (s32[24,128]{1,0:T(8,128)S(1)}, s32[1]{0:T(128)}) custom-call(s32[4,64]{1,0:T(4,128)} %bitcast.9, s32[1,64]{1,0:T(1,128)} %bitcast.10), custom_call_target="tpu_custom_call" | custom-call | tf_op jit(solution)/shard_map/pallas_call | solution.py:97
  2.9 94.3 %conditional.1 = (bf16[768,512]{1,0:T(8,128)(2,1)S(1)}, bf16[768,512]{1,0:T(8,128)(2,1)S(1)}, f32[]{:T(128)}) conditional(s32[]{:T(128)} %bitcast.6, (s32[24,128]{1,0:T(8,128)S(1)}, bf16[24,8192]{1,0:T(8,128)(2,1)}, bf16[8192,512]{1,0:T(8,128)(2,1)}, bf16[768,512]{1,0:T(8,128)(2,1)}, bf16[8,256,256]{2,1,0:T(8,128)(2,1)}, ...), branch_computations={%region_0.0_spmd, %region_1.0_spmd, %region_2.0_spmd, %region_3.0_... | conditional | flops 8000000000 | bytes 20971544 | solution.py:453
  2.9 94.0 %branch_0_fun.1 = (bf16[768,512]{1,0:T(8,128)(2,1)S(1)}, bf16[768,512]{1,0:T(8,128)(2,1)S(1)}, f32[1]{0:T(128)}) custom-call(s32[24,128]{1,0:T(8,128)S(1)} %get-tuple-element.69.plan, bf16[24,8192]{1,0:T(8,128)(2,1)} %get-tuple-element.70.a_ref, bf16[8192,512]{1,0:T(8,128)(2,1)} %get-tuple-element.71.b_ref, bf16[768,512]{1,0:T(8,128)(2,1)} %get-tuple-element.72.amp_ref, ...), custom_call_target="tpu_custom_call" | custom-call | flops 8000000000 | bytes 20971520 | tf_op jit(solution)/shard_map/cond/branch_0_fun/pallas_call | solution.py:419
  97.2 0.9 copy.30
  98.1 0.9 copy.31

commit v4 on v3

--- a/solution.py
+++ b/solution.py
@@ -10,7 +10,7 @@
 MESH = pl.DeviceIdType.MESH
 RING = 4
 DIST = (1, 3, 2)
-CAPS = ((6, 5), (6, 6), (8, 8), (16, 16))
+CAPS = ((5, 5), (6, 5), (6, 6), (8, 8), (16, 16))
 PART = 2048
 F32, BF16 = jnp.float32, jnp.bfloat16
 
@@ -292,10 +292,10 @@
     pass_on(0)
     own_b.wait()
     arrived("amp")
-    multiply(0,0,2)
+    multiply(0, 0, 2)
     pass_on(3)
     arrived("b")
-    multiply(0,2,2)
+    multiply(0, 2, 2)
     pass_on(1)
     own_l.wait()
     arrived("l")
@@ -313,14 +313,16 @@
     share(0, 1)
     for i in range(RING):
         arrived(("a2", i, 1, 1))
-    multiply(3,0,4)
+    multiply(3, 0, 2)
     share(3, 0)
+    multiply(3, 2, 2)
     share(3, 1)
     share_on(0)
     for i in range(RING):
         arrived(("a2", i, -1, 0))
-    multiply(1,0,4)
+    multiply(1, 0, 2)
     share(1, 0)
+    multiply(1, 2, 2)
     share(1, 1)
     share_on(3)
     share_on(1)
@@ -328,10 +330,10 @@
         arrived(("a2r", i, 1))
         arrived(("a2r", i, -1))
     hand_out(0)
-    multiply(2,0,2)
-    share(2,0)
-    multiply(2,2,2)
-    share(2,1)
+    multiply(2, 0, 2)
+    share(2, 0)
+    multiply(2, 2, 2)
+    share(2, 1)
     hand_out(3)
     hand_out(1)
     share_on(2)
@@ -339,30 +341,36 @@
 
     nacc[...] = jnp.zeros_like(nacc)
 
-    def finish(j):
-        for g, d in enumerate(DIST):
-            arrived(("e2", (j - d) % RING, DIST.index((-d) % RING)))
-        row = (q + j) % RING
+    def finish(*chunks):
+        for j in chunks:
+            for g, d in enumerate(DIST):
+                arrived(("e2", (j - d) % RING, DIST.index((-d) % RING)))
 
         def one_tile(t, carry):
             cols = pl.ds(pl.multiple_of((t % 2) * 256, 256), 256)
-            total = jnp.zeros((96, 256), F32)
+            total = jnp.zeros((96 * len(chunks), 256), F32)
             for k in range(4):
-                near = rows[j][plan[4 + k, mine + t]].astype(F32)
-                far = got[j][plan[8 + k, mine + t]].astype(F32)
-                block = jnp.where(plan[12 + k, mine + t] == 1, near, far).astype(BF16)
+                parts = []
+                for j in chunks:
+                    near = rows[j][plan[4 + k, mine + t]].astype(F32)
+                    far = got[j][plan[8 + k, mine + t]].astype(F32)
+                    parts.append(jnp.where(plan[12 + k, mine + t] == 1, near, far).astype(BF16))
+                block = jnp.concatenate(parts, axis=0)
                 total += jnp.dot(block, lbuf[t // 2, (t % 2) * 4 + k], preferred_element_type=F32)
-            residual = (total + cyc[j, t].astype(F32)).astype(BF16)
-            wide = residual.astype(F32)
-            resbuf[t // 2, row, :, cols] = residual
-            nacc[...] += (wide * wide).reshape(12, 8, 256).sum(axis=0)
+            for n, j in enumerate(chunks):
+                residual = (total[96 * n : 96 * n + 96] + cyc[j, t].astype(F32)).astype(BF16)
+                wide = residual.astype(F32)
+                resbuf[t // 2, (q + j) % RING, :, cols] = residual
+                nacc[...] += (wide * wide).reshape(12, 8, 256).sum(axis=0)
             return carry
 
         lax.fori_loop(0, 4, one_tile, 0)
-        send(("res", j), resbuf.at[sister, row], resin.at[row], to_sister)
-
-    for j in (2, 0, 3, 1):
-        finish(j)
+        for j in chunks:
+            row = (q + j) % RING
+            send(("res", j), resbuf.at[sister, row], resin.at[row], to_sister)
+
+    finish(2)
+    finish(0, 3, 1)
 
     def write(first, last):
         def rows_of(cc, fq, fp):
@@ -381,7 +389,7 @@
             new_ref[here, :] = (amp_ref[here, :].astype(F32) - block / denom).astype(BF16)
 
     def spread_norm(stage, slot, value, devices):
-        nbuf[stage, slot] = jnp.full((8, 128), value, F32)
+        nbuf[stage, slot] = value
         for n, dev in enumerate(devices):
             send(("n", stage, n), nbuf.at[stage, slot], nbuf.at[stage, slot], dev)
 
@@ -391,16 +399,19 @@
         total = nbuf[stage, 0]
         for n in range(1, len(devices) + 1):
             total = total + nbuf[stage, n]
-        return jnp.max(total)
-
-    spread_norm(0, z * 2 + core, jnp.sum(nacc[...]), group)
+        return total
+
+    earlier = list(made.values())
+    spread_norm(0, z * 2 + core, nacc[:, 0:128] + nacc[:, 128:256], group)
     for j in range(RING):
         arrived(("res", j))
     write(0, 8)
+    for one in earlier:
+        one.wait_send()
     spread_norm(1, p * 4 + q, sum_norm(0, group), plane)
     write(8, 16)
-    norm_ref[0] = sum_norm(1, plane)
-    for one in made.values():
+    norm_ref[0] = jnp.sum(sum_norm(1, plane))
+    for one in list(made.values())[len(earlier) :]:
         one.wait_send()
 
 

time: 101 us -> 101 us (level)
  no operation moved by 1% of the time
where the time goes in v4:
time: 101 us
  Pallas kernels  95.8 us (95%)
  between operations  3.05 us (3%)
  local copies, waits for them, and re-layouts  1.76 us (2%)
    pallas_call x1, Pallas kernels, run_main(): pl.pallas_call(functools.partial(main, caps, width), out_shape=(out, out,...  94.3 us

profile of v4, /device:TPU:1, one launch (start us, length us, event | category | flops | bytes accessed | tf_op | source)
XLA Modules:
  0.0 101.2 jit_solution(3042638477794284221)
XLA Ops:
  0.6 1.6 %shard_map.108 = (s32[24,128]{1,0:T(8,128)S(1)}, s32[1]{0:T(128)}) custom-call(s32[4,64]{1,0:T(4,128)} %bitcast.10, s32[1,64]{1,0:T(1,128)} %bitcast.11), custom_call_target="tpu_custom_call" | custom-call | tf_op jit(solution)/shard_map/pallas_call | solution.py:97
  2.9 94.8 %conditional.1 = (bf16[768,512]{1,0:T(8,128)(2,1)S(1)}, bf16[768,512]{1,0:T(8,128)(2,1)S(1)}, f32[]{:T(128)}) conditional(s32[]{:T(128)} %bitcast.7, (s32[24,128]{1,0:T(8,128)S(1)}, bf16[24,8192]{1,0:T(8,128)(2,1)}, bf16[8192,512]{1,0:T(8,128)(2,1)}, bf16[768,512]{1,0:T(8,128)(2,1)}, bf16[8,256,256]{2,1,0:T(8,128)(2,1)}, ...), branch_computations={%region_0.0_spmd, %region_1.0_spmd, %region_2.0_spmd, %region_3.0_... | conditional | flops 8000000000 | bytes 20971544 | solution.py:464
  3.1 94.3 %branch_2_fun.1 = (bf16[768,512]{1,0:T(8,128)(2,1)S(1)}, bf16[768,512]{1,0:T(8,128)(2,1)S(1)}, f32[1]{0:T(128)}) custom-call(s32[24,128]{1,0:T(8,128)S(1)} %get-tuple-element.106.plan, bf16[24,8192]{1,0:T(8,128)(2,1)} %get-tuple-element.107.a_ref, bf16[8192,512]{1,0:T(8,128)(2,1)} %get-tuple-element.108.b_ref, bf16[768,512]{1,0:T(8,128)(2,1)} %get-tuple-element.109.amp_ref, ...), custom_call_target="tpu_custom_call" | custom-call | flops 8000000000 | bytes 20971520 | tf_op jit(solution)/shard_map/cond/branch_2_fun/pallas_call | solution.py:430
  97.7 0.9 copy.34
  98.6 0.9 copy.35

commit v5 on v4

--- a/solution.py
+++ b/solution.py
@@ -10,7 +10,7 @@
 MESH = pl.DeviceIdType.MESH
 RING = 4
 DIST = (1, 3, 2)
-CAPS = ((5, 5), (6, 5), (6, 6), (8, 8), (16, 16))
+CAPS = ((5, 5), (6, 5), (6, 6), (7, 7), (8, 8), (16, 16))
 PART = 2048
 F32, BF16 = jnp.float32, jnp.bfloat16
 
@@ -133,11 +133,13 @@
 
     made = {}
 
-    def send(key, src, dst, dev):
-        n = len(made)
-        made[key] = pltpu.make_async_remote_copy(
+    def describe(n, src, dst, dev):
+        return pltpu.make_async_remote_copy(
             src_ref=src, dst_ref=dst, send_sem=ssem.at[n], recv_sem=rsem.at[n], device_id=dev, device_id_type=MESH
         )
+
+    def send(key, src, dst, dev):
+        made[key] = describe(len(made), src, dst, dev)
         made[key].start()
 
     def arrived(key):
@@ -225,7 +227,7 @@
     arrived(("a1r", -1))
     spread(2)
 
-    def multiply(j, first, tiles):
+    def multiply(j, then=lambda n: None):
         row = (q + j) % RING
 
         def one_tile(n, carry):
@@ -257,12 +259,28 @@
             rows[j][p * 4 + t] = (amps + cycle.astype(F32)).astype(BF16)
             return carry
 
-        lax.fori_loop(first, first + tiles, one_tile, 0)
-
-    def share(j, n):
-        two = pl.ds(p * 4 + 2 * ((core + n) % 2), 2)
-        for way in (1, -1):
-            send(("e1", j, way, n), rows[j].at[two], rows[j].at[two], at(p + way, q))
+        def two_tiles(n, carry):
+            lax.fori_loop(2 * n, 2 * n + 2, one_tile, 0)
+            then(n)
+            return carry
+
+        lax.fori_loop(0, 2, two_tiles, 0)
+
+    def share(j):
+        base = len(made)
+
+        def both_ways(n):
+            two = pl.ds(p * 4 + 2 * ((core + n) % 2), 2)
+            return [describe(base + 2 * n + w, rows[j].at[two], rows[j].at[two], at(p + way, q)) for w, way in enumerate((1, -1))]
+
+        for n in range(2):
+            made["e1", j, 1, n], made["e1", j, -1, n] = both_ways(n)
+
+        def start(n):
+            for one in both_ways(n):
+                one.start()
+
+        return start
 
     def share_on(j):
         for n, way, source in ((0, 1, pm), (1, -1, pp)):
@@ -292,10 +310,9 @@
     pass_on(0)
     own_b.wait()
     arrived("amp")
-    multiply(0, 0, 2)
     pass_on(3)
     arrived("b")
-    multiply(0, 2, 2)
+    multiply(0)
     pass_on(1)
     own_l.wait()
     arrived("l")
@@ -309,31 +326,23 @@
 
     lax.fori_loop(0, 16, mask_weights, 0)
     pass_on(2)
-    share(0, 0)
-    share(0, 1)
+    start = share(0)
+    start(0)
+    start(1)
     for i in range(RING):
         arrived(("a2", i, 1, 1))
-    multiply(3, 0, 2)
-    share(3, 0)
-    multiply(3, 2, 2)
-    share(3, 1)
+    multiply(3, share(3))
     share_on(0)
     for i in range(RING):
         arrived(("a2", i, -1, 0))
-    multiply(1, 0, 2)
-    share(1, 0)
-    multiply(1, 2, 2)
-    share(1, 1)
+    multiply(1, share(1))
     share_on(3)
     share_on(1)
     for i in range(RING):
         arrived(("a2r", i, 1))
         arrived(("a2r", i, -1))
     hand_out(0)
-    multiply(2, 0, 2)
-    share(2, 0)
-    multiply(2, 2, 2)
-    share(2, 1)
+    multiply(2, share(2))
     hand_out(3)
     hand_out(1)
     share_on(2)

time: 101 us -> 106 us (1.050)
  Pallas kernels: 95.8 us -> 100 us
    pallas_call x1, Pallas kernels: 94.3 us -> 98.5 us  [run_main(): pl.pallas_call(functools.partial(main, caps, width), out_shape=(out, out,...]
where the time goes in v5:
time: 106 us; the launch traced here: 105 us
  Pallas kernels  100 us (94%)
  between operations  2.99 us (3%)
  local copies, waits for them, and re-layouts  1.76 us (2%)
    pallas_call x1, Pallas kernels, run_main(): pl.pallas_call(functools.partial(main, caps, width), out_shape=(out, out,...  98.5 us

profile of v5, /device:TPU:1, one launch (start us, length us, event | category | flops | bytes accessed | tf_op | source)
XLA Modules:
  0.0 105.4 jit_solution(1970914956796302050)
XLA Ops:
  0.6 1.6 %shard_map.109 = (s32[24,128]{1,0:T(8,128)S(1)}, s32[1]{0:T(128)}) custom-call(s32[4,64]{1,0:T(4,128)} %bitcast.11, s32[1,64]{1,0:T(1,128)} %bitcast.12), custom_call_target="tpu_custom_call" | custom-call | tf_op jit(solution)/shard_map/pallas_call | solution.py:97
  2.9 99.0 %conditional.1 = (bf16[768,512]{1,0:T(8,128)(2,1)S(1)}, bf16[768,512]{1,0:T(8,128)(2,1)S(1)}, f32[]{:T(128)}) conditional(s32[]{:T(128)} %bitcast.8, (s32[24,128]{1,0:T(8,128)S(1)}, bf16[24,8192]{1,0:T(8,128)(2,1)}, bf16[8192,512]{1,0:T(8,128)(2,1)}, bf16[768,512]{1,0:T(8,128)(2,1)}, bf16[8,256,256]{2,1,0:T(8,128)(2,1)}, ...), branch_computations={%region_0.0_spmd, %region_1.0_spmd, %region_2.0_spmd, %region_3.0_... | conditional | flops 8000000000 | bytes 20971544 | solution.py:473
  3.1 98.5 %branch_3_fun.1 = (bf16[768,512]{1,0:T(8,128)(2,1)S(1)}, bf16[768,512]{1,0:T(8,128)(2,1)S(1)}, f32[1]{0:T(128)}) custom-call(s32[24,128]{1,0:T(8,128)S(1)} %get-tuple-element.133.plan, bf16[24,8192]{1,0:T(8,128)(2,1)} %get-tuple-element.134.a_ref, bf16[8192,512]{1,0:T(8,128)(2,1)} %get-tuple-element.135.b_ref, bf16[768,512]{1,0:T(8,128)(2,1)} %get-tuple-element.136.amp_ref, ...), custom_call_target="tpu_custom_call" | custom-call | flops 8000000000 | bytes 20971520 | tf_op jit(solution)/shard_map/cond/branch_3_fun/pallas_call | solution.py:439
  101.9 0.9 copy.38
  102.8 0.9 copy.39

commit v6 on v5

--- a/solution.py
+++ b/solution.py
@@ -10,7 +10,7 @@
 MESH = pl.DeviceIdType.MESH
 RING = 4
 DIST = (1, 3, 2)
-CAPS = ((5, 5), (6, 5), (6, 6), (7, 7), (8, 8), (16, 16))
+CAPS = ((5, 5), (6, 5), (5, 6), (6, 6), (7, 7), (8, 8), (16, 16))
 PART = 2048
 F32, BF16 = jnp.float32, jnp.bfloat16
 

time: 106 us -> 104 us (0.981); the launches traced: 105 us -> 105 us
  no operation moved by 1% of the time
where the time goes in v6:
time: 104 us; the launch traced here: 105 us
  Pallas kernels  100 us (96%)
  between operations  3.05 us (3%)
  local copies, waits for them, and re-layouts  1.76 us (2%)
    pallas_call x1, Pallas kernels, run_main(): pl.pallas_call(functools.partial(main, caps, width), out_shape=(out, out,...  98.5 us

profile of v6, /device:TPU:1, one launch (start us, length us, event | category | flops | bytes accessed | tf_op | source)
XLA Modules:
  0.0 105.4 jit_solution(15393092976794778636)
XLA Ops:
  0.6 1.6 %shard_map.110 = (s32[24,128]{1,0:T(8,128)S(1)}, s32[1]{0:T(128)}) custom-call(s32[4,64]{1,0:T(4,128)} %bitcast.12, s32[1,64]{1,0:T(1,128)} %bitcast.13), custom_call_target="tpu_custom_call" | custom-call | tf_op jit(solution)/shard_map/pallas_call | solution.py:97
  2.9 99.0 %conditional.1 = (bf16[768,512]{1,0:T(8,128)(2,1)S(1)}, bf16[768,512]{1,0:T(8,128)(2,1)S(1)}, f32[]{:T(128)}) conditional(s32[]{:T(128)} %bitcast.9, (s32[24,128]{1,0:T(8,128)S(1)}, bf16[24,8192]{1,0:T(8,128)(2,1)}, bf16[8192,512]{1,0:T(8,128)(2,1)}, bf16[768,512]{1,0:T(8,128)(2,1)}, bf16[8,256,256]{2,1,0:T(8,128)(2,1)}, ...), branch_computations={%region_0.0_spmd, %region_1.0_spmd, %region_2.0_spmd, %region_3.0_... | conditional | flops 8000000000 | bytes 20971544 | solution.py:473
  3.1 98.5 %branch_4_fun.1 = (bf16[768,512]{1,0:T(8,128)(2,1)S(1)}, bf16[768,512]{1,0:T(8,128)(2,1)S(1)}, f32[1]{0:T(128)}) custom-call(s32[24,128]{1,0:T(8,128)S(1)} %get-tuple-element.160.plan, bf16[24,8192]{1,0:T(8,128)(2,1)} %get-tuple-element.161.a_ref, bf16[8192,512]{1,0:T(8,128)(2,1)} %get-tuple-element.162.b_ref, bf16[768,512]{1,0:T(8,128)(2,1)} %get-tuple-element.163.amp_ref, ...), custom_call_target="tpu_custom_call" | custom-call | flops 8000000000 | bytes 20971520 | tf_op jit(solution)/shard_map/cond/branch_4_fun/pallas_call | solution.py:439
  101.9 0.9 copy.42
  102.8 0.9 copy.43
